TPU v7x, 32 devices: a whole 2x2x4 slice. The times are simulated.
32 devices in a mesh: ctx: 8 (over y, x, core), exp: 4 (over z).
Axes of the slice: x: 2, y: 2, z: 4, core: 2. Of those that a mesh axis runs over, the one named last changes fastest.
Arguments:
- ssm_input: bfloat16 [1024, 4096], P('ctx', 'exp'), may hold values from -6 to 6
- gate_input: bfloat16 [1024, 4096], P('ctx', 'exp'), may hold values from -6 to 6
- key_proj: bfloat16 [1024, 128], P('ctx'), may hold values from -4 to 4
- query_proj: bfloat16 [1024, 128], P('ctx'), may hold values from -4 to 4
- step_size: float32 [1024, 64], P('ctx', 'exp'), may hold values from 0 to 1, as said below
- decay_rate: float32 [64], P('exp'), may hold values from 0.5 to 1.5
- head_gain: float32 [4096], P('exp'), may hold values from 0.5 to 1.5
- residual: bfloat16 [1024, 4096], P('ctx', 'exp'), may hold values from -33 to 33
- ffn_gain: float32 [4096], replicated, may hold values from 0.5 to 1.5
- gate_weight: bfloat16 [4, 4096, 12288], P('exp', None, 'ctx'), may hold values from -0.09375 to 0.09375
- up_weight: bfloat16 [4, 4096, 12288], P('exp', None, 'ctx'), may hold values from -0.09375 to 0.09375
- down_weight: bfloat16 [4, 12288, 4096], P('exp', 'ctx'), may hold values from -0.0546875 to 0.0546875
- expert_ids: int32 [1024, 2], P('ctx'), may hold values from 0 to 3, all different within a row; in each aligned block of 128 rows (0 to 127, 128 to 255, ...) at most 96 rows name the same one
- route_weight: float32 [1024, 2], P('ctx'), may hold values from 0.5 to 2
Outputs:
- block_out: bfloat16 [1024, 4096], P('ctx', 'exp')
- expert_out: bfloat16 [1024, 4096], P('ctx', 'exp')
Inputs may be any that keep to these rules, and one draw needn't show every extreme that they name: `step_size`: step sizes are positive. `expert_ids`: the two experts of a token differ. In each aligned block of 128 rows (the tokens of one shard) no expert is named by more than 96 rows, and in some block one expert is named by exactly 96 rows.
All inputs are finite; a program needn't handle non-finite values.
Results may differ from a plain program's by a relative error of at most 0.022.
Values may be sent and summed in bfloat16 or wider, within the bound.
A program may use at most 128 MiB of HBM per device.

v0:
```python
import jax
import jax.numpy as jnp
from jax import lax
from jax.sharding import PartitionSpec as P

precise = lax.Precision.HIGHEST


def carried_in(shard, axis, combine, identity):
    length, mine = (lax.axis_size(axis), lax.axis_index(axis))
    everything = jax.tree.map(
        lambda part, kind: lax.all_gather(part.astype(kind), axis),
        shard,
        (jnp.bfloat16, jnp.bfloat16),
    )
    start = jax.tree.map(
        lambda part, zero: jnp.broadcast_to(jnp.asarray(zero, part.dtype), part.shape),
        shard,
        identity,
    )

    def lap(k, before):
        reached = k < mine
        new = combine(
            before, jax.tree.map(lambda part, own: part[k].astype(own.dtype), everything, shard)
        )
        return jax.tree.map(lambda a, b: jnp.where(reached, a, b), new, before)

    return lax.fori_loop(0, length, lap, start)


def local_block(ssm_piece, key_piece, query_piece, step_piece, decay_rate, head_count):
    row_count = ssm_piece.shape[0]
    head_width = ssm_piece.shape[1] // head_count
    values = ssm_piece.astype(jnp.float32).reshape(row_count, head_count, head_width)
    key_vals = key_piece.astype(jnp.float32)
    queries = query_piece.astype(jnp.float32)
    log_steps = -step_piece * decay_rate[None, :]
    running = jnp.cumsum(log_steps, axis=0)
    scores = jnp.dot(queries, key_vals.T, precision=precise)
    causal = (jnp.arange(row_count)[:, None] >= jnp.arange(row_count)[None, :])[:, :, None]
    spacing = running[:, None, :] - running[None, :, :]
    decays = jnp.where(causal, jnp.exp(jnp.where(causal, spacing, 0.0)), 0.0)
    within = jnp.einsum("tsh,ts,shp->thp", decays, scores, values, precision=precise)
    overall = running[-1]
    fading = jnp.exp(overall[None, :] - running)
    states = jnp.einsum("sh,shp,sn->hpn", fading, values, key_vals, precision=precise)
    return (within, running, overall, states)


def route_tables(expert_ids, route_weight, experts, capacity):
    matched = expert_ids[None, :, :] == experts[:, None, None]
    member = jnp.any(matched, axis=2).astype(jnp.int32)
    gate_sum = jnp.sum(jnp.where(matched, route_weight[None, :, :], 0.0), axis=2)
    slot_index = jnp.cumsum(member, axis=1) - 1
    positions = jnp.arange(capacity, dtype=jnp.int32)
    routing = (
        (slot_index[:, None, :] == positions[None, :, None]) & (member[:, None, :] > 0)
    ).astype(jnp.float32)
    slot_weight = jnp.einsum("nkt,nt->nk", routing, gate_sum, precision=precise)
    return (routing, slot_weight)


def join_states(earlier, later):
    return (earlier[0] + later[0], jnp.exp(later[0])[:, None, None] * earlier[1] + later[1])


def on_device(
    ssm_input,
    gate_input,
    key_proj,
    query_proj,
    step_size,
    decay_rate,
    head_gain,
    residual,
    ffn_gain,
    gate_weight,
    up_weight,
    down_weight,
    expert_ids,
    route_weight,
):
    head_count = step_size.shape[1]
    row_count, channels = ssm_input.shape
    head_width = channels // head_count
    within, running, overall, states = local_block(
        ssm_input, key_proj, query_proj, step_size, decay_rate, head_count
    )
    prefix = carried_in(
        (overall, states), "ctx", join_states, (jnp.zeros_like(overall), jnp.zeros_like(states))
    )
    before = prefix[1]
    carried = jnp.einsum(
        "th,hpn,tn->thp",
        jnp.exp(running),
        before,
        query_proj.astype(jnp.float32),
        precision=precise,
    )
    mixer_out = within + carried
    gated_out = mixer_out * jax.nn.silu(gate_input.astype(jnp.float32)).reshape(
        row_count, head_count, head_width
    )
    inv_rms = lax.rsqrt(jnp.mean(gated_out * gated_out, axis=2, keepdims=True) + 1e-05)
    normed = (gated_out * inv_rms).reshape(row_count, channels) * head_gain[None, :]
    block_out = (residual.astype(jnp.float32) + normed).astype(jnp.bfloat16)
    owner_index = lax.axis_index("exp")
    exp_count = lax.axis_size("exp")
    capacity = 3 * row_count // exp_count
    tables, weights_all = route_tables(
        expert_ids, route_weight, jnp.arange(exp_count, dtype=jnp.int32), capacity
    )
    own_table = lax.dynamic_index_in_dim(tables, owner_index, 0, keepdims=False)
    own_weight = lax.dynamic_index_in_dim(weights_all, owner_index, 0, keepdims=False)
    gathered = lax.all_gather(block_out, "exp", axis=1, tiled=True)
    widened = gathered.astype(jnp.float32)
    ffn_input = (
        widened
        * lax.rsqrt(jnp.mean(widened * widened, axis=1, keepdims=True) + 1e-06)
        * ffn_gain[None, :]
    ).astype(jnp.bfloat16)
    chosen = jnp.dot(
        own_table.astype(jnp.bfloat16), ffn_input, preferred_element_type=jnp.float32
    ).astype(jnp.bfloat16)
    gate_here = gate_weight[0]
    up_here = up_weight[0]
    down_here = down_weight[0]
    token_piece = lax.all_gather(chosen, "ctx", axis=0, tiled=True)
    gate_proj = jnp.dot(token_piece, gate_here, preferred_element_type=jnp.float32)
    up_proj = jnp.dot(token_piece, up_here, preferred_element_type=jnp.float32)
    hidden = (jax.nn.silu(gate_proj) * up_proj).astype(jnp.bfloat16)
    summed = lax.psum_scatter(
        jnp.dot(hidden, down_here, preferred_element_type=jnp.float32).astype(jnp.bfloat16),
        "ctx",
        scatter_dimension=0,
        tiled=True,
    )
    spread = jnp.dot(
        own_table.T, own_weight[:, None] * summed.astype(jnp.float32), precision=precise
    )
    expert_out = lax.psum_scatter(
        spread.astype(jnp.bfloat16), "exp", scatter_dimension=1, tiled=True
    )
    return (block_out, expert_out)


def solution(mesh):
    placed = (
        P("ctx", "exp"),
        P("ctx", "exp"),
        P("ctx", None),
        P("ctx", None),
        P("ctx", "exp"),
        P("exp"),
        P("exp"),
        P("ctx", "exp"),
        P(),
        P("exp", None, "ctx"),
        P("exp", None, "ctx"),
        P("exp", "ctx", None),
        P("ctx", None),
        P("ctx", None),
    )
    return jax.shard_map(
        on_device,
        mesh=mesh,
        in_specs=placed,
        out_specs=(P("ctx", "exp"), P("ctx", "exp")),
        check_vma=False,
    )
```

profile of v0, /device:TPU:24, one launch (start us, length us, event | category | flops | bytes accessed | tf_op | source)
XLA Modules:
  0.0 273.8 jit_solution(5218710078034619074)
XLA Ops:
  7.2 0.0 all-gather.10.cloned.1.call-start
  7.2 0.8 negate_multiply_fusion
  8.0 0.1 copy.47
  8.1 0.2 reduce_window_sum.22
  8.3 0.1 copy.52
  8.4 1.1 copy.50
  9.5 1.1 convolution_convert_fusion.2
  10.6 0.0 all-gather.10.cloned.1.call-update
  10.6 0.0 all-gather.6.cloned.1.call-start
  10.7 0.1 copy.48
  10.8 8.8 %all-gather.1 = bf16[8,1,16]{2,1,0:T(2,128)(2,1)S(1)} all-gather(bf16[1,1,16]{2,1,0:T(2,128)(2,1)S(1)} %convert_bitcast_fusion), channel_id=1, replica_groups=mesh['ctx'=8,'exp'=4] {'ctx'}, dimensions={0}, use_global_device_ids=true | all-gather | bytes 288 | tf_op jit(solution)/shard_map/all_gather | solution.py:12
  19.6 1.1 convert_multiply_fusion.2
  20.7 0.2 copy.53
  20.9 0.9 fusion.55
  21.8 17.8 %all-gather.10.cloned.1.call-done = bf16[128,64,128]{2,1,0:T(8,128)(2,1)} async-done(((bf16[16,64,128]{2,1,0:T(8,128)(2,1)}), bf16[128,64,128]{2,1,0:T(8,128)(2,1)}) %all-gather.10.cloned.1.call-update) | async-done | bytes 2097168 | tf_op jit(solution)/shard_map/all_gather | solution.py:12
  39.7 9.1 %while.14 = (s32[]{:T(128)}, f32[16,64,128]{2,1,0:T(8,128)S(1)}, s32[]{:T(128)}, bf16[8,16]{1,0:T(8,128)(2,1)S(1)}, bf16[8,16,64,128]{3,2,1,0:T(8,128)(2,1)}, /*index=5*/s32[]{:T(128)}, s32[]{:T(128)}) while((s32[]{:T(128)}, f32[16,64,128]{2,1,0:T(8,128)S(1)}, s32[]{:T(128)}, bf16[8,16]{1,0:T(8,128)(2,1)S(1)}, ...), condition=%wide.region_2.3_spmd.clone, body=%wide.region_1.2_spmd.clone.sunk | while | flops 655380 | bytes 1310985 | solution.py:29
  39.7 1.1 fusion.66
  40.9 1.1 fusion.66
  42.0 1.1 fusion.66
  43.1 1.1 fusion.66
  44.3 1.1 fusion.66
  45.4 1.1 fusion.66
  46.6 1.1 fusion.66
  47.7 1.1 fusion.66
  48.8 0.4 fusion.21
  49.2 1.4 multiply_reduce_fusion
  50.7 0.2 copy.54
  50.9 0.8 add_convert_fusion
  51.7 0.0 all-gather.6.cloned.1.call-update
  51.7 0.0 all-gather.8.cloned.1.call-start
  51.8 0.3 reduce_window_sum.23
  52.2 26.2 %all-gather.6.cloned.1.call-done = bf16[128,4096]{1,0:T(8,128)(2,1)} async-done(((bf16[128,1024]{1,0:T(8,128)(2,1)}), bf16[128,4096]{1,0:T(8,128)(2,1)}) %all-gather.6.cloned.1.call-update) | async-done | bytes 1048592 | tf_op jit(solution)/shard_map/all_gather | solution.py:116
  78.4 1.5 fusion.14
  79.9 2.6 convolution_convert_fusion.1
  82.5 0.0 all-gather.8.cloned.1.call-update
  82.6 0.2 reduce-scatter.3.cloned.1.call-start
  82.8 46.4 %all-gather.8.cloned.1.call-done = bf16[768,4096]{1,0:T(8,128)(2,1)} async-done(((bf16[96,4096]{1,0:T(8,128)(2,1)}), bf16[768,4096]{1,0:T(8,128)(2,1)}) %all-gather.8.cloned.1.call-update) | async-done | bytes 6291472 | tf_op jit(solution)/shard_map/all_gather | solution.py:129
  129.2 16.1 %fusion.3 = f32[768,1536]{1,0:T(8,128)} fusion(bf16[768,4096]{1,0:T(8,128)(2,1)} %all-gather.8.cloned.1.call-done, bf16[1,4096,1536]{2,1,0:T(8,128)(2,1)} %param.26), kind=kOutput, calls=%fused_computation.5 | convolution fusion | flops 9663676416 | bytes 23592960 | tf_op jit(solution)/shard_map/dot_general | solution.py:131
  145.3 31.7 %fusion.7 = bf16[768,4096]{1,0:T(8,128)(2,1)} fusion(bf16[1,1536,4096]{2,1,0:T(8,128)(2,1)} %param.27, f32[768,1536]{1,0:T(8,128)} %fusion.3, bf16[768,4096]{1,0:T(8,128)(2,1)} %all-gather.8.cloned.1.call-done, bf16[1,4096,1536]{2,1,0:T(8,128)(2,1)} %param.25), kind=kOutput, calls=%fused_computation.9 | convolution fusion | flops 19337576448 | bytes 42467328 | tf_op jit(solution)/shard_map/dot_general | solution.py:134
  177.0 0.0 reduce-scatter.3.cloned.1.call-update
  177.0 0.0 reduce-scatter.5.cloned.1.call-start
  177.0 0.6 copy-done.7
  177.7 0.1 copy-done.3
  177.8 0.2 fusion.56
  178.0 60.9 %reduce-scatter.3.cloned.1.call-done = bf16[96,4096]{1,0:T(8,128)(2,1)} async-done(((bf16[768,4096]{1,0:T(8,128)(2,1)}), bf16[96,4096]{1,0:T(8,128)(2,1)}) %reduce-scatter.3.cloned.1.call-update) | async-done | bytes 786448 | tf_op jit(solution)/shard_map/reduce_scatter | solution.py:133
  238.9 3.3 %convolution_convert_fusion = bf16[128,4096]{1,0:T(8,128)(2,1)} fusion(bf16[96,4096]{1,0:T(8,128)(2,1)} %reduce-scatter.3.cloned.1.call-done, f32[96]{0:T(128)S(1)} %dynamic-slice_bitcast_fusion, pred[4,96,128]{2,1,0:T(32,128)(4,1)S(1)} %copy-done.3, s32[]{:T(128)S(6)} %select_n.41), kind=kOutput, calls=%fused_computation.10 | convolution fusion | flops 605290496 | bytes 1847812 | tf_op jit(solution)/shard_map/dot_general | solution.py:139
  242.2 0.0 reduce-scatter.5.cloned.1.call-update
  242.3 25.0 %reduce-scatter.5.cloned.1.call-done = bf16[128,1024]{1,0:T(8,128)(2,1)} async-done(((bf16[128,4096]{1,0:T(8,128)(2,1)}), bf16[128,1024]{1,0:T(8,128)(2,1)}) %reduce-scatter.5.cloned.1.call-update) | async-done | bytes 262160 | tf_op jit(solution)/shard_map/reduce_scatter | solution.py:142
  (42 shorter events, 0.4 us)
Async XLA Ops:
  7.2 2.3 copy-start
  7.2 32.5 %all-gather.10.cloned.1.call-start = ((), (), s32[]{:S(2)}) async-start(), calls=%async_computation.6 | async-start | bytes 2359296 | tf_op jit(solution)/shard_map/all_gather | solution.py:12
  10.6 38.2 %copy-start.4 = (bf16[128,128]{1,0:T(8,128)(2,1)S(1)}, bf16[128,128]{1,0:T(8,128)(2,1)}, u32[]{:S(2)}) copy-start(bf16[128,128]{1,0:T(8,128)(2,1)} %param.19) | copy-start | bytes 98308
  10.6 67.7 %all-gather.6.cloned.1.call-start = ((), (), s32[]{:S(2)}) async-start(), calls=%async_computation.2 | async-start | bytes 1310720 | tf_op jit(solution)/shard_map/all_gather | solution.py:116
  39.7 11.2 %copy-start.1 = (bf16[128,1024]{1,0:T(8,128)(2,1)S(1)}, bf16[128,1024]{1,0:T(8,128)(2,1)}, u32[]{:S(2)}) copy-start(bf16[128,1024]{1,0:T(8,128)(2,1)} %param.23) | copy-start | bytes 786436
  39.7 11.2 %copy-start.5 = (f32[1024]{0:T(1024)S(1)}, f32[1024]{0:T(1024)}, u32[]{:S(2)}) copy-start(f32[1024]{0:T(1024)} %param.22) | copy-start | bytes 12292
  48.8 3.0 %copy-start.6 = (s32[128,2]{0,1:T(2,128)S(1)}, s32[128,2]{0,1:T(2,128)}, u32[]{:S(2)}) copy-start(s32[128,2]{0,1:T(2,128)} %param.28) | copy-start | bytes 3076
  48.8 31.1 %copy-start.9 = (f32[4096]{0:T(1024)S(1)}, f32[4096]{0:T(1024)}, u32[]{:S(2)}) copy-start(f32[4096]{0:T(1024)} %param.24) | copy-start | bytes 49156
  51.7 77.4 %all-gather.8.cloned.1.call-start = ((), (), s32[]{:S(2)}) async-start(), calls=%async_computation.3 | async-start | bytes 7077888 | tf_op jit(solution)/shard_map/all_gather | solution.py:129
  52.2 93.1 %copy-start.2 = (pred[4,96,128]{2,1,0:T(32,128)(4,1)}, pred[4,96,128]{2,1,0:T(32,128)(4,1)S(1)}, u32[]{:S(2)}) copy-start(pred[4,96,128]{2,1,0:T(32,128)(4,1)S(1)} %fusion.42) | copy-start | bytes 147460
  82.6 156.3 %reduce-scatter.3.cloned.1.call-start = ((), (), s32[]{:S(2)}) async-start(), calls=%async_computation.4 | async-start | bytes 7077888 | tf_op jit(solution)/shard_map/reduce_scatter | solution.py:133
  177.0 0.7 copy-start.7
  177.0 0.7 copy-start.8
  177.0 0.8 copy-start.3
  177.0 90.3 %reduce-scatter.5.cloned.1.call-start = ((), (), s32[]{:S(2)}) async-start(), calls=%async_computation.5 | async-start | bytes 1310720 | tf_op jit(solution)/shard_map/reduce_scatter | solution.py:142
Sparse Core Ops, SparseCore 0:
  10.8 28.8 all-gather.9
  51.8 26.4 all-gather.5
  82.7 46.4 all-gather.7
  177.1 61.7 reduce-scatter.2
  242.4 24.8 reduce-scatter.4
where the time goes:
time: 279 us; the launch traced here: 274 us
  waiting for transfers between devices  176 us (63%)
  matrix products  57.7 us (21%)
  between operations  14 us (5%)
  other arithmetic  13.8 us (5%)
  blocking collectives  8.76 us (3%)
    reduce_scatter x1, waiting for transfers between devices, on_device(): lax.psum_scatter(jnp.dot(hidden, down_here, preferred_element_type=jnp.fl...  60.9 us
    all_gather x1, waiting for transfers between devices, on_device(): token_piece = lax.all_gather(chosen, 'ctx', axis=0, tiled=True)  46.4 us
    dot_general x1, matrix products, on_device(): jnp.dot(hidden, down_here, preferred_element_type=jnp.float32)  31.7 us
    all_gather x1, waiting for transfers between devices, on_device(): gathered = lax.all_gather(block_out, 'exp', axis=1, tiled=True)  26.2 us
    reduce_scatter x1, waiting for transfers between devices, on_device(): lax.psum_scatter(spread.astype(jnp.bfloat16), 'exp', scatter_dimension=1,...  25 us
    all_gather x1, waiting for transfers between devices, carried_in(): lax.all_gather(part.astype(kind), axis)  17.8 us
    dot_general x1, matrix products, on_device(): up_proj = jnp.dot(token_piece, up_here, preferred_element_type=jnp.float32)  16.1 us
    select_n x8, other arithmetic, lap(): return jax.tree.map(lambda a, b: jnp.where(reached, a, b), new, before)  8.82 us
  transfers between devices with their start and end apart: 5, of which 5 were waited for; matrix products, arithmetic and copies ran while one was open for 1% of the time, Pallas kernels for 0%

commit v1 on v0

--- a/solution.py
+++ b/solution.py
@@ -1,6 +1,11 @@
+import functools
+import math
+
 import jax
 import jax.numpy as jnp
 from jax import lax
+from jax.experimental import pallas as pl
+from jax.experimental.pallas import tpu as pltpu
 from jax.sharding import PartitionSpec as P
 
 precise = lax.Precision.HIGHEST
@@ -57,8 +62,329 @@
     routing = (
         (slot_index[:, None, :] == positions[None, :, None]) & (member[:, None, :] > 0)
     ).astype(jnp.float32)
-    slot_weight = jnp.einsum("nkt,nt->nk", routing, gate_sum, precision=precise)
-    return (routing, slot_weight)
+    return (routing, gate_sum)
+
+
+MESH = pl.DeviceIdType.MESH
+
+
+def expert_kernel(
+    wide,
+    tall,
+    picked_ref,
+    gain_ref,
+    gate_hbm,
+    up_hbm,
+    down_hbm,
+    out_ref,
+    arrived,
+    rows_ref,
+    gate_ref,
+    up_ref,
+    down_ref,
+    hidden_ref,
+    pair_ref,
+    first_ref,
+    second_ref,
+    leaving,
+    load_sem,
+    in_sem,
+    one_sem,
+    two_sem,
+    twin_sem,
+    swap_sem,
+    fold_sem,
+    last_sem,
+    out_sem,
+):
+    me, z = lax.axis_index("ctx"), lax.axis_index("exp")
+    planes, count, width = picked_ref.shape
+    half = rows_ref.shape[3]
+    depth = gate_ref.shape[1]
+    model = gate_ref.shape[0]
+    core = lax.rem(me, 2)
+    chip = me // 2
+    x, y = lax.rem(chip, wide), chip // wide
+    sizes = (wide, tall)
+
+    def chip_at(i, j):
+        return lax.rem(y + j + tall, tall) * wide + lax.rem(x + i + wide, wide)
+
+    def ctx_at(i, j):
+        return chip_at(i, j) * 2 + core
+
+    def send(source, target, sem, index, where):
+        return pltpu.make_async_remote_copy(
+            src_ref=source,
+            dst_ref=target,
+            send_sem=sem.at[(0,) + index],
+            recv_sem=sem.at[(1,) + index],
+            device_id=where,
+            device_id_type=MESH,
+        )
+
+    def along(h, first, second):
+        return (first, second) if h == 0 else (second, first)
+
+    twin = {"ctx": me + 1 - 2 * core}
+    partners = [twin]
+    partners += [{"ctx": ctx_at(i, 0)} for i in range(1, wide)]
+    partners += [{"ctx": ctx_at(0, j)} for j in range(1, tall)]
+    partners += [{"exp": lax.rem(z + d, planes)} for d in range(1, planes)]
+    barrier = pltpu.get_barrier_semaphore()
+    for partner in partners:
+        pl.semaphore_signal(barrier, inc=1, device_id=partner, device_id_type=MESH)
+    pl.semaphore_wait(barrier, len(partners))
+
+    inward = []
+    for d in range(1, planes):
+        goal = lax.rem(z + d, planes)
+        inward.append(send(picked_ref.at[goal], arrived.at[z], in_sem, (d,), {"exp": goal}))
+        inward[-1].start()
+    loads = [
+        pltpu.make_async_copy(gate_hbm, gate_ref, load_sem.at[0]),
+        pltpu.make_async_copy(up_hbm, up_ref, load_sem.at[1]),
+        pltpu.make_async_copy(down_hbm, down_ref, load_sem.at[2]),
+    ]
+    for load in loads:
+        load.start()
+    arrived[z] = picked_ref[z]
+    for copy in inward:
+        copy.wait_recv()
+    total = jnp.zeros((count, 1), jnp.float32)
+    for s in range(planes):
+        part = arrived[s].astype(jnp.float32)
+        total = total + jnp.sum(part * part, axis=1, keepdims=True)
+    scale = lax.rsqrt(total / model + 1e-06)
+    for s in range(planes):
+        h, start = (s * width) // half, (s * width) % half
+        rows_ref[h, me, :, start : start + width] = (
+            arrived[s].astype(jnp.float32) * scale * gain_ref[s : s + 1, :]
+        ).astype(jnp.bfloat16)
+
+    ones, twos, twins = {}, {}, {}
+    for h in range(2):
+        major, minor = along(h, wide, tall)
+        for k in range(1, major):
+            i, j = along(h, k, 0)
+            block = rows_ref.at[h, me]
+            ones[h, k] = send(block, block, one_sem, (h, k), {"ctx": ctx_at(i, j)})
+            ones[h, k].start()
+
+    def pass_on(h, i, j):
+        block = rows_ref.at[h, ctx_at(-i, -j)]
+        twins[h, i, j] = send(block, block, twin_sem, (h, i, j), twin)
+        twins[h, i, j].start()
+
+    def turn(h, k):
+        major, minor = along(h, wide, tall)
+        i, j = along(h, k, 0)
+        block = rows_ref.at[h, ctx_at(-i, -j)]
+        for m in range(1, minor):
+            a, b = along(h, 0, m)
+            twos[h, k, m] = send(block, block, two_sem, (h, k, m), {"ctx": ctx_at(a, b)})
+            twos[h, k, m].start()
+
+    for h in range(2):
+        turn(h, 0)
+    for h in range(2):
+        pass_on(h, 0, 0)
+
+    step = 256 if depth % 256 == 0 else 128
+
+    def raise_rows(i, j):
+        group = j * wide + i
+        blocks = pl.ds(chip_at(-i, -j) * 2, 2)
+
+        @pl.loop(0, depth // step)
+        def _(t):
+            cols = pl.ds(pl.multiple_of(t * step, step), step)
+
+            def product(w_ref):
+                value = None
+                for h in range(2):
+                    left = rows_ref[h, blocks].reshape(2 * count, half)
+                    term = jnp.dot(
+                        left,
+                        w_ref[h * half : (h + 1) * half, cols],
+                        preferred_element_type=jnp.float32,
+                    )
+                    value = term if value is None else value + term
+                return value
+
+            gate = product(gate_ref)
+            hidden_ref[group, :, cols] = (gate * jax.nn.sigmoid(gate) * product(up_ref)).astype(
+                jnp.bfloat16
+            )
+
+    order = sorted(
+        [(i, j) for i in range(wide) for j in range(tall)], key=lambda o: (o[0] + o[1], o)
+    )
+    loads[0].wait()
+    loads[1].wait()
+    for h in range(2):
+        twins[h, 0, 0].wait_recv()
+    raise_rows(0, 0)
+    for h in range(2):
+        for k in range(1, sizes[h]):
+            ones[h, k].wait_recv()
+            turn(h, k)
+            i, j = along(h, k, 0)
+            pass_on(h, i, j)
+    for h in range(2):
+        for m in range(1, sizes[1 - h]):
+            twos[h, 0, m].wait_recv()
+            i, j = along(h, 0, m)
+            pass_on(h, i, j)
+    for i, j in order[1:]:
+        for h in range(2):
+            k, m = along(h, i, j)
+            if k > 0 and m > 0:
+                twos[h, k, m].wait_recv()
+                pass_on(h, i, j)
+        for h in range(2):
+            twins[h, i, j].wait_recv()
+        raise_rows(i, j)
+    for copy in list(ones.values()) + list(twos.values()) + list(twins.values()):
+        copy.wait_send()
+
+    swaps, folds, lasts = {}, {}, {}
+    loads[2].wait()
+
+    def lower_rows(i, j):
+        group = lax.rem(tall - j, tall) * wide + lax.rem(wide - i, wide)
+        group = ((tall - j) % tall) * wide + (wide - i) % wide
+        base = chip_at(i, j) * 2
+        for h in range(2):
+
+            @pl.loop(0, half // 256)
+            def _(t):
+                cols = pl.ds(pl.multiple_of(t * 256, 256), 256)
+                source = pl.ds(pl.multiple_of(h * half + t * 256, 256), 256)
+                value = jnp.dot(
+                    hidden_ref[group], down_ref[:, source], preferred_element_type=jnp.float32
+                )
+                rows_ref[h, pl.ds(base, 2), :, cols] = value.astype(jnp.bfloat16).reshape(
+                    2, count, 256
+                )
+
+            swaps[h, i, j] = send(
+                rows_ref.at[h, base + 1 - core],
+                pair_ref.at[h, j * wide + i],
+                swap_sem,
+                (h, i, j),
+                twin,
+            )
+            swaps[h, i, j].start()
+
+    def add_into(target, other):
+        @pl.loop(0, count // 16)
+        def _(t):
+            some = pl.ds(pl.multiple_of(t * 16, 16), 16)
+            target[some, :] = (
+                target[some, :].astype(jnp.float32) + other[some, :].astype(jnp.float32)
+            ).astype(jnp.bfloat16)
+
+    def settle(i, j):
+        for h in range(2):
+            swaps[h, i, j].wait_recv()
+            own = rows_ref.at[h, ctx_at(i, j)]
+            add_into(own, pair_ref.at[h, j * wide + i])
+            k, m = along(h, i, j)
+            if k > 0:
+                a, b = along(h, k, 0)
+                folds[h, k, m] = send(
+                    own, first_ref.at[h, k, m], fold_sem, (h, k, m), {"ctx": ctx_at(a, b)}
+                )
+                folds[h, k, m].start()
+
+    goals = order[::-1]
+    for number, goal in enumerate(goals):
+        lower_rows(*goal)
+        if number:
+            settle(*goals[number - 1])
+    settle(*goals[-1])
+    for h in range(2):
+        major, minor = along(h, wide, tall)
+        for m in list(range(1, minor)) + [0]:
+            i, j = along(h, 0, m)
+            own = rows_ref.at[h, ctx_at(i, j)]
+            for k in range(1, major):
+                folds[h, k, m].wait_recv()
+                add_into(own, first_ref.at[h, k, m])
+            if m:
+                lasts[h, m] = send(
+                    own, second_ref.at[h, m], last_sem, (h, m), {"ctx": ctx_at(i, j)}
+                )
+                lasts[h, m].start()
+    for h in range(2):
+        for m in range(1, sizes[1 - h]):
+            lasts[h, m].wait_recv()
+            add_into(rows_ref.at[h, me], second_ref.at[h, m])
+    for s in range(planes):
+        h, start = (s * width) // half, (s * width) % half
+        leaving[s] = rows_ref[h, me, :, start : start + width]
+    outward = []
+    for d in range(1, planes):
+        goal = lax.rem(z + d, planes)
+        outward.append(send(leaving.at[goal], out_ref.at[z], out_sem, (d,), {"exp": goal}))
+        outward[-1].start()
+    out_ref[z] = leaving[z]
+    for copy in outward:
+        copy.wait_recv()
+    for copy in inward + outward + list(swaps.values()) + list(folds.values()):
+        copy.wait_send()
+    for copy in lasts.values():
+        copy.wait_send()
+
+
+def expert_rows(picked, gain, gate_here, up_here, down_here):
+    shards, planes = lax.axis_size("ctx"), lax.axis_size("exp")
+    chips = shards // 2
+    wide = math.isqrt(chips)
+    tall = chips // wide
+    _, count, width = picked.shape
+    model, depth = gate_here.shape
+    half = model // 2
+    most = max(wide, tall)
+    vmem = pl.BlockSpec(memory_space=pltpu.VMEM)
+    hbm = pl.BlockSpec(memory_space=pl.ANY)
+    sems = pltpu.SemaphoreType.DMA
+    return pl.pallas_call(
+        functools.partial(expert_kernel, wide, tall),
+        out_shape=jax.ShapeDtypeStruct((planes, count, width), jnp.bfloat16),
+        in_specs=[vmem, vmem, hbm, hbm, hbm],
+        out_specs=vmem,
+        scratch_shapes=[
+            pltpu.VMEM((planes, count, width), jnp.bfloat16),
+            pltpu.VMEM((2, shards, count, half), jnp.bfloat16),
+            pltpu.VMEM((model, depth), jnp.bfloat16),
+            pltpu.VMEM((model, depth), jnp.bfloat16),
+            pltpu.VMEM((depth, model), jnp.bfloat16),
+            pltpu.VMEM((chips, 2 * count, depth), jnp.bfloat16),
+            pltpu.VMEM((2, chips, count, half), jnp.bfloat16),
+            pltpu.VMEM((2, most, most, count, half), jnp.bfloat16),
+            pltpu.VMEM((2, most, count, half), jnp.bfloat16),
+            pltpu.VMEM((planes, count, width), jnp.bfloat16),
+            sems((3,)),
+            sems((2, planes)),
+            sems((2, 2, most)),
+            sems((2, 2, most, most)),
+            sems((2, 2, wide, tall)),
+            sems((2, 2, wide, tall)),
+            sems((2, 2, most, most)),
+            sems((2, 2, most)),
+            sems((2, planes)),
+        ],
+        compiler_params=pltpu.CompilerParams(
+            collective_id=0, has_side_effects=True, vmem_limit_bytes=60 * 1024 * 1024
+        ),
+        cost_estimate=pl.CostEstimate(
+            flops=6 * shards * count * model * depth,
+            bytes_accessed=6 * model * depth,
+            transcendentals=shards * count * depth,
+        ),
+    )(picked, gain, gate_here, up_here, down_here)
 
 
 def join_states(earlier, later):
@@ -105,43 +431,31 @@
     inv_rms = lax.rsqrt(jnp.mean(gated_out * gated_out, axis=2, keepdims=True) + 1e-05)
     normed = (gated_out * inv_rms).reshape(row_count, channels) * head_gain[None, :]
     block_out = (residual.astype(jnp.float32) + normed).astype(jnp.bfloat16)
-    owner_index = lax.axis_index("exp")
     exp_count = lax.axis_size("exp")
     capacity = 3 * row_count // exp_count
-    tables, weights_all = route_tables(
+    tables, gate_sum = route_tables(
         expert_ids, route_weight, jnp.arange(exp_count, dtype=jnp.int32), capacity
     )
-    own_table = lax.dynamic_index_in_dim(tables, owner_index, 0, keepdims=False)
-    own_weight = lax.dynamic_index_in_dim(weights_all, owner_index, 0, keepdims=False)
-    gathered = lax.all_gather(block_out, "exp", axis=1, tiled=True)
-    widened = gathered.astype(jnp.float32)
-    ffn_input = (
-        widened
-        * lax.rsqrt(jnp.mean(widened * widened, axis=1, keepdims=True) + 1e-06)
-        * ffn_gain[None, :]
+    rows = exp_count * capacity
+    picked = jnp.dot(
+        tables.reshape(rows, row_count).astype(jnp.bfloat16),
+        block_out,
+        preferred_element_type=jnp.float32,
     ).astype(jnp.bfloat16)
-    chosen = jnp.dot(
-        own_table.astype(jnp.bfloat16), ffn_input, preferred_element_type=jnp.float32
-    ).astype(jnp.bfloat16)
-    gate_here = gate_weight[0]
-    up_here = up_weight[0]
-    down_here = down_weight[0]
-    token_piece = lax.all_gather(chosen, "ctx", axis=0, tiled=True)
-    gate_proj = jnp.dot(token_piece, gate_here, preferred_element_type=jnp.float32)
-    up_proj = jnp.dot(token_piece, up_here, preferred_element_type=jnp.float32)
-    hidden = (jax.nn.silu(gate_proj) * up_proj).astype(jnp.bfloat16)
-    summed = lax.psum_scatter(
-        jnp.dot(hidden, down_here, preferred_element_type=jnp.float32).astype(jnp.bfloat16),
-        "ctx",
-        scatter_dimension=0,
-        tiled=True,
-    )
-    spread = jnp.dot(
-        own_table.T, own_weight[:, None] * summed.astype(jnp.float32), precision=precise
-    )
-    expert_out = lax.psum_scatter(
-        spread.astype(jnp.bfloat16), "exp", scatter_dimension=1, tiled=True
-    )
+    returned = expert_rows(
+        picked.reshape(exp_count, capacity, channels),
+        ffn_gain.reshape(exp_count, channels),
+        gate_weight[0],
+        up_weight[0],
+        down_weight[0],
+    )
+    spread = jnp.einsum(
+        "ekt,ekf->etf",
+        tables.astype(jnp.bfloat16),
+        returned,
+        preferred_element_type=jnp.float32,
+    )
+    expert_out = jnp.sum(spread * gate_sum[:, :, None], axis=0).astype(jnp.bfloat16)
     return (block_out, expert_out)
 
 

time: 279 us -> 184 us (0.66); the launches traced: 274 us -> 183 us
  waiting for transfers between devices: 176 us -> 18.5 us
  Pallas kernels: 0 us -> 121 us
  matrix products: 57.7 us -> 6.59 us
  other arithmetic: 13.8 us -> 10.7 us
    pallas_call x0 -> x1, Pallas kernels: none -> 121 us  [expert_rows(): pl.pallas_call(functools.partial(expert_kernel, wide, tall), out_shape=ja...]
    reduce_scatter x2 -> x0, waiting for transfers between devices: 85.9 us -> none  [the longest x1 60.9 us: on_device(): lax.psum_scatter(jnp.dot(hidden, down_here, preferred_element_type=jnp.fl...]
    all_gather x2 -> x0, waiting for transfers between devices: 72.6 us -> none  [the longest x1 46.4 us: on_device(): token_piece = lax.all_gather(chosen, 'ctx', axis=0, tiled=True)]
    dot_general x5 -> x2, matrix products: 54 us -> 3.62 us  [the longest x1 2.39 us: on_device(): jnp.einsum('ekt,ekf->etf', tables.astype(jnp.bfloat16), returned, preferr...]
  transfers between devices with their start and end apart: 5 -> 1, of which waited for: 5 -> 1; matrix products, arithmetic and copies ran while one was open for 1% -> 1% of each run, Pallas kernels for 0% -> 0%
where the time goes in v1:
time: 184 us; the launch traced here: 183 us
  Pallas kernels  121 us (66%)
  waiting for transfers between devices  18.5 us (10%)
  between operations  14.3 us (8%)
  other arithmetic  10.7 us (6%)
  blocking collectives  8.76 us (5%)
  matrix products  6.59 us (4%)
  local copies, waits for them, and re-layouts  2.54 us (1%)
    pallas_call x1, Pallas kernels, expert_rows(): pl.pallas_call(functools.partial(expert_kernel, wide, tall), out_shape=ja...  121 us
    all_gather x1, waiting for transfers between devices, carried_in(): lax.all_gather(part.astype(kind), axis)  18.5 us
    select_n x8, other arithmetic, lap(): return jax.tree.map(lambda a, b: jnp.where(reached, a, b), new, before)  8.78 us
    all_gather x1, blocking collectives, carried_in(): lax.all_gather(part.astype(kind), axis)  8.76 us
  transfers between devices with their start and end apart: 1, of which 1 were waited for; matrix products, arithmetic and copies ran while one was open for 1% of the time, Pallas kernels for 0%

profile of v1, /device:TPU:24, one launch (start us, length us, event | category | flops | bytes accessed | tf_op | source)
XLA Modules:
  0.0 183.0 jit_solution(3251289169084646597)
XLA Ops:
  7.2 0.0 copy-start
  7.2 0.0 copy-start.2
  7.2 0.0 copy-start.7
  7.2 0.0 copy-start.5
  7.2 0.0 copy-start.8
  7.2 0.0 copy-start.4
  7.2 0.0 all-gather.4.cloned.1.call-start
  7.3 0.8 negate_multiply_fusion
  8.1 0.1 copy.47
  8.2 0.2 reduce_window_sum.22
  8.4 0.1 copy.52
  8.5 1.1 copy.50
  9.6 0.0 copy-done
  9.6 1.1 convolution_convert_fusion.1
  10.7 0.0 all-gather.4.cloned.1.call-update
  10.8 0.1 copy.48
  10.8 8.8 %all-gather.1 = bf16[8,1,16]{2,1,0:T(2,128)(2,1)S(1)} all-gather(bf16[1,1,16]{2,1,0:T(2,128)(2,1)S(1)} %convert_bitcast_fusion), channel_id=1, replica_groups=mesh['ctx'=8,'exp'=4] {'ctx'}, dimensions={0}, use_global_device_ids=true | all-gather | bytes 288 | tf_op jit(solution)/shard_map/all_gather | solution.py:17
  19.6 0.0 copy-done.2
  19.6 0.2 convert_multiply_fusion
  19.8 0.2 copy.53
  20.0 0.0 copy-done.7
  20.0 0.3 reduce_window_sum.23
  20.3 0.1 eq.45
  20.4 0.0 copy-done.5
  20.4 0.6 reshape.80.gain_ref
  21.0 0.1 convert_convert_fusion
  21.2 0.0 copy-done.4
  21.2 0.1 fusion.29
  21.4 18.5 %all-gather.4.cloned.1.call-done = bf16[128,64,128]{2,1,0:T(8,128)(2,1)} async-done(((bf16[16,64,128]{2,1,0:T(8,128)(2,1)}), bf16[128,64,128]{2,1,0:T(8,128)(2,1)}) %all-gather.4.cloned.1.call-update) | async-done | bytes 2097168 | tf_op jit(solution)/shard_map/all_gather | solution.py:17
  39.8 9.1 %while.14 = (s32[]{:T(128)}, f32[16,64,128]{2,1,0:T(8,128)S(1)}, s32[]{:T(128)}, bf16[8,16]{1,0:T(8,128)(2,1)S(1)}, bf16[8,16,64,128]{3,2,1,0:T(8,128)(2,1)}, /*index=5*/s32[]{:T(128)}, s32[]{:T(128)}) while((s32[]{:T(128)}, f32[16,64,128]{2,1,0:T(8,128)S(1)}, s32[]{:T(128)}, bf16[8,16]{1,0:T(8,128)(2,1)S(1)}, ...), condition=%wide.region_2.3_spmd.clone, body=%wide.region_1.2_spmd.clone.sunk | while | flops 655380 | bytes 1310985 | solution.py:34
  39.8 1.1 fusion.38
  41.0 1.1 fusion.38
  42.1 1.1 fusion.38
  43.3 1.1 fusion.38
  44.4 1.1 fusion.38
  45.5 1.1 fusion.38
  46.7 1.1 fusion.38
  47.8 1.1 fusion.38
  48.9 0.4 fusion.3
  49.3 0.0 copy-start.3
  49.3 0.0 copy-start.6
  49.3 1.4 multiply_reduce_fusion.1
  50.8 0.2 copy.54
  51.0 0.1 add_convert_fusion
  51.1 0.0 copy-start.1
  51.1 1.2 convolution_convert_fusion
  52.3 121.5 %shard_map.149 = bf16[4,96,1024]{2,1,0:T(8,128)(2,1)} custom-call(bf16[4,96,1024]{2,1,0:T(8,128)(2,1)} %bitcast.59, f32[4,1024]{1,0:T(4,128)} %reshape.80.gain_ref, bf16[4096,1536]{1,0:T(8,128)(2,1)} %bitcast.62, bf16[4096,1536]{1,0:T(8,128)(2,1)} %bitcast.63, bf16[1536,4096]{1,0:T(8,128)(2,1)} %bitcast.64), custom_call_target="tpu_custom_call" | custom-call | flops 28991029248 | bytes 37748736 | tf_op jit(solution)/shard_map/pallas_call | solution.py:353
  173.8 2.4 %multiply_reduce_fusion = bf16[128,1024]{1,0:T(8,128)(2,1)} fusion(bf16[4,96,1024]{2,1,0:T(8,128)(2,1)} %shard_map.149, f32[4,128]{1,0:T(4,128)S(1)} %select_reduce_fusion, s32[4,128]{1,0:T(4,128)S(1)} %broadcast_add_fusion, pred[4,128]{1,0:T(4,128)(4,1)S(1)} %get-tuple-element.127), kind=kOutput, calls=%fused_computation.3 | convolution fusion | flops 101777408 | bytes 1053184 | tf_op jit(solution)/shard_map/ekt,ekf->etf/dot_general | solution.py:452
  (26 shorter events, 0.3 us)
Async XLA Ops:
  7.2 2.4 %copy-start = (bf16[128,128]{1,0:T(8,128)(2,1)S(1)}, bf16[128,128]{1,0:T(8,128)(2,1)}, u32[]{:S(2)}) copy-start(bf16[128,128]{1,0:T(8,128)(2,1)} %param.18) | copy-start | bytes 98308
  7.2 12.4 %copy-start.2 = (bf16[128,1024]{1,0:T(8,128)(2,1)S(1)}, bf16[128,1024]{1,0:T(8,128)(2,1)}, u32[]{:S(2)}) copy-start(bf16[128,1024]{1,0:T(8,128)(2,1)} %param.17) | copy-start | bytes 786436
  7.2 12.8 %copy-start.7 = (s32[128,2]{0,1:T(2,128)S(1)}, s32[128,2]{0,1:T(2,128)}, u32[]{:S(2)}) copy-start(s32[128,2]{0,1:T(2,128)} %param.28) | copy-start | bytes 3076
  7.2 13.2 %copy-start.5 = (f32[4096]{0:T(1024)S(1)}, f32[4096]{0:T(1024)}, u32[]{:S(2)}) copy-start(f32[4096]{0:T(1024)} %param.24) | copy-start | bytes 49156
  7.2 14.0 %copy-start.8 = (f32[128,2]{0,1:T(2,128)S(1)}, f32[128,2]{0,1:T(2,128)}, u32[]{:S(2)}) copy-start(f32[128,2]{0,1:T(2,128)} %param.29) | copy-start | bytes 3076
  7.2 14.0 %copy-start.4 = (bf16[128,128]{1,0:T(8,128)(2,1)S(1)}, bf16[128,128]{1,0:T(8,128)(2,1)}, u32[]{:S(2)}) copy-start(bf16[128,128]{1,0:T(8,128)(2,1)} %param.19) | copy-start | bytes 98308
  7.2 32.6 %all-gather.4.cloned.1.call-start = ((), (), s32[]{:S(2)}) async-start(), calls=%async_computation | async-start | bytes 2359296 | tf_op jit(solution)/shard_map/all_gather | solution.py:17
  49.3 1.7 copy-start.3
  49.3 1.7 copy-start.6
  51.1 122.7 %copy-start.1 = (bf16[128,1024]{1,0:T(8,128)(2,1)}, bf16[128,1024]{1,0:T(8,128)(2,1)S(1)}, u32[]{:S(2)}) copy-start(bf16[128,1024]{1,0:T(8,128)(2,1)S(1)} %add_convert_fusion) | copy-start | bytes 786436
Sparse Core Ops, SparseCore 0:
  10.9 28.9 all-gather.3

commit v2 on v1

--- a/solution.py
+++ b/solution.py
@@ -9,29 +9,6 @@
 from jax.sharding import PartitionSpec as P
 
 precise = lax.Precision.HIGHEST
-
-
-def carried_in(shard, axis, combine, identity):
-    length, mine = (lax.axis_size(axis), lax.axis_index(axis))
-    everything = jax.tree.map(
-        lambda part, kind: lax.all_gather(part.astype(kind), axis),
-        shard,
-        (jnp.bfloat16, jnp.bfloat16),
-    )
-    start = jax.tree.map(
-        lambda part, zero: jnp.broadcast_to(jnp.asarray(zero, part.dtype), part.shape),
-        shard,
-        identity,
-    )
-
-    def lap(k, before):
-        reached = k < mine
-        new = combine(
-            before, jax.tree.map(lambda part, own: part[k].astype(own.dtype), everything, shard)
-        )
-        return jax.tree.map(lambda a, b: jnp.where(reached, a, b), new, before)
-
-    return lax.fori_loop(0, length, lap, start)
 
 
 def local_block(ssm_piece, key_piece, query_piece, step_piece, decay_rate, head_count):
@@ -106,6 +83,8 @@
     chip = me // 2
     x, y = lax.rem(chip, wide), chip // wide
     sizes = (wide, tall)
+    pieces = 2 if count % 32 == 0 else 1
+    piece = count // pieces
 
     def chip_at(i, j):
         return lax.rem(y + j + tall, tall) * wide + lax.rem(x + i + wide, wide)
@@ -136,11 +115,21 @@
         pl.semaphore_signal(barrier, inc=1, device_id=partner, device_id_type=MESH)
     pl.semaphore_wait(barrier, len(partners))
 
-    inward = []
-    for d in range(1, planes):
-        goal = lax.rem(z + d, planes)
-        inward.append(send(picked_ref.at[goal], arrived.at[z], in_sem, (d,), {"exp": goal}))
-        inward[-1].start()
+    def some(r):
+        return pl.ds(r * piece, piece)
+
+    inward = {}
+    for r in range(pieces):
+        for d in range(1, planes):
+            goal = lax.rem(z + d, planes)
+            inward[d, r] = send(
+                picked_ref.at[goal, some(r)],
+                arrived.at[z, some(r)],
+                in_sem,
+                (d, r),
+                {"exp": goal},
+            )
+            inward[d, r].start()
     loads = [
         pltpu.make_async_copy(gate_hbm, gate_ref, load_sem.at[0]),
         pltpu.make_async_copy(up_hbm, up_ref, load_sem.at[1]),
@@ -149,46 +138,48 @@
     for load in loads:
         load.start()
     arrived[z] = picked_ref[z]
-    for copy in inward:
-        copy.wait_recv()
-    total = jnp.zeros((count, 1), jnp.float32)
-    for s in range(planes):
-        part = arrived[s].astype(jnp.float32)
-        total = total + jnp.sum(part * part, axis=1, keepdims=True)
-    scale = lax.rsqrt(total / model + 1e-06)
-    for s in range(planes):
-        h, start = (s * width) // half, (s * width) % half
-        rows_ref[h, me, :, start : start + width] = (
-            arrived[s].astype(jnp.float32) * scale * gain_ref[s : s + 1, :]
-        ).astype(jnp.bfloat16)
-
     ones, twos, twins = {}, {}, {}
-    for h in range(2):
-        major, minor = along(h, wide, tall)
-        for k in range(1, major):
-            i, j = along(h, k, 0)
-            block = rows_ref.at[h, me]
-            ones[h, k] = send(block, block, one_sem, (h, k), {"ctx": ctx_at(i, j)})
-            ones[h, k].start()
-
-    def pass_on(h, i, j):
-        block = rows_ref.at[h, ctx_at(-i, -j)]
-        twins[h, i, j] = send(block, block, twin_sem, (h, i, j), twin)
-        twins[h, i, j].start()
-
-    def turn(h, k):
-        major, minor = along(h, wide, tall)
+
+    def pass_on(h, i, j, r):
+        block = rows_ref.at[h, ctx_at(-i, -j), some(r)]
+        twins[h, i, j, r] = send(block, block, twin_sem, (h, i, j, r), twin)
+        twins[h, i, j, r].start()
+
+    def turn(h, k, r):
         i, j = along(h, k, 0)
-        block = rows_ref.at[h, ctx_at(-i, -j)]
-        for m in range(1, minor):
+        block = rows_ref.at[h, ctx_at(-i, -j), some(r)]
+        for m in range(1, sizes[1 - h]):
             a, b = along(h, 0, m)
-            twos[h, k, m] = send(block, block, two_sem, (h, k, m), {"ctx": ctx_at(a, b)})
-            twos[h, k, m].start()
-
-    for h in range(2):
-        turn(h, 0)
-    for h in range(2):
-        pass_on(h, 0, 0)
+            twos[h, k, m, r] = send(
+                block, block, two_sem, (h, k, m, r), {"ctx": ctx_at(a, b)}
+            )
+            twos[h, k, m, r].start()
+
+    for r in range(pieces):
+        for d in range(1, planes):
+            inward[d, r].wait_recv()
+        total = jnp.zeros((piece, 1), jnp.float32)
+        for s in range(planes):
+            part = arrived[s, some(r)].astype(jnp.float32)
+            total = total + jnp.sum(part * part, axis=1, keepdims=True)
+        scale = lax.rsqrt(total / model + 1e-06)
+        for s in range(planes):
+            h, start = (s * width) // half, (s * width) % half
+            rows_ref[h, me, some(r), start : start + width] = (
+                arrived[s, some(r)].astype(jnp.float32) * scale * gain_ref[s : s + 1, :]
+            ).astype(jnp.bfloat16)
+        for h in range(2):
+            for k in range(1, sizes[h]):
+                i, j = along(h, k, 0)
+                block = rows_ref.at[h, me, some(r)]
+                ones[h, k, r] = send(
+                    block, block, one_sem, (h, k, r), {"ctx": ctx_at(i, j)}
+                )
+                ones[h, k, r].start()
+        for h in range(2):
+            turn(h, 0, r)
+        for h in range(2):
+            pass_on(h, 0, 0, r)
 
     step = 256 if depth % 256 == 0 else 128
 
@@ -222,28 +213,38 @@
     )
     loads[0].wait()
     loads[1].wait()
-    for h in range(2):
-        twins[h, 0, 0].wait_recv()
+    for r in range(pieces):
+        for h in range(2):
+            for k in range(1, sizes[h]):
+                if r == 0:
+                    ones[h, k, r].wait_recv()
+                    turn(h, k, r)
+                    pass_on(h, *along(h, k, 0), r)
+    for r in range(pieces):
+        for h in range(2):
+            twins[h, 0, 0, r].wait_recv()
     raise_rows(0, 0)
-    for h in range(2):
-        for k in range(1, sizes[h]):
-            ones[h, k].wait_recv()
-            turn(h, k)
-            i, j = along(h, k, 0)
-            pass_on(h, i, j)
-    for h in range(2):
-        for m in range(1, sizes[1 - h]):
-            twos[h, 0, m].wait_recv()
-            i, j = along(h, 0, m)
-            pass_on(h, i, j)
+    for r in range(1, pieces):
+        for h in range(2):
+            for k in range(1, sizes[h]):
+                ones[h, k, r].wait_recv()
+                turn(h, k, r)
+                pass_on(h, *along(h, k, 0), r)
+    for r in range(pieces):
+        for h in range(2):
+            for m in range(1, sizes[1 - h]):
+                twos[h, 0, m, r].wait_recv()
+                pass_on(h, *along(h, 0, m), r)
     for i, j in order[1:]:
-        for h in range(2):
-            k, m = along(h, i, j)
-            if k > 0 and m > 0:
-                twos[h, k, m].wait_recv()
-                pass_on(h, i, j)
-        for h in range(2):
-            twins[h, i, j].wait_recv()
+        for r in range(pieces):
+            for h in range(2):
+                k, m = along(h, i, j)
+                if k > 0 and m > 0:
+                    twos[h, k, m, r].wait_recv()
+                    pass_on(h, i, j, r)
+        for r in range(pieces):
+            for h in range(2):
+                twins[h, i, j, r].wait_recv()
         raise_rows(i, j)
     for copy in list(ones.values()) + list(twos.values()) + list(twins.values()):
         copy.wait_send()
@@ -252,7 +253,6 @@
     loads[2].wait()
 
     def lower_rows(i, j):
-        group = lax.rem(tall - j, tall) * wide + lax.rem(wide - i, wide)
         group = ((tall - j) % tall) * wide + (wide - i) % wide
         base = chip_at(i, j) * 2
         for h in range(2):
@@ -278,25 +278,31 @@
             swaps[h, i, j].start()
 
     def add_into(target, other):
-        @pl.loop(0, count // 16)
+        @pl.loop(0, piece // 16)
         def _(t):
-            some = pl.ds(pl.multiple_of(t * 16, 16), 16)
-            target[some, :] = (
-                target[some, :].astype(jnp.float32) + other[some, :].astype(jnp.float32)
+            few = pl.ds(pl.multiple_of(t * 16, 16), 16)
+            target[few, :] = (
+                target[few, :].astype(jnp.float32) + other[few, :].astype(jnp.float32)
             ).astype(jnp.bfloat16)
 
     def settle(i, j):
         for h in range(2):
             swaps[h, i, j].wait_recv()
-            own = rows_ref.at[h, ctx_at(i, j)]
-            add_into(own, pair_ref.at[h, j * wide + i])
-            k, m = along(h, i, j)
-            if k > 0:
-                a, b = along(h, k, 0)
-                folds[h, k, m] = send(
-                    own, first_ref.at[h, k, m], fold_sem, (h, k, m), {"ctx": ctx_at(a, b)}
-                )
-                folds[h, k, m].start()
+        for r in range(pieces):
+            for h in range(2):
+                own = rows_ref.at[h, ctx_at(i, j), some(r)]
+                add_into(own, pair_ref.at[h, j * wide + i, some(r)])
+                k, m = along(h, i, j)
+                if k > 0:
+                    a, b = along(h, k, 0)
+                    folds[h, k, m, r] = send(
+                        own,
+                        first_ref.at[h, k, m, some(r)],
+                        fold_sem,
+                        (h, k, m, r),
+                        {"ctx": ctx_at(a, b)},
+                    )
+                    folds[h, k, m, r].start()
 
     goals = order[::-1]
     for number, goal in enumerate(goals):
@@ -304,38 +310,52 @@
         if number:
             settle(*goals[number - 1])
     settle(*goals[-1])
-    for h in range(2):
-        major, minor = along(h, wide, tall)
-        for m in list(range(1, minor)) + [0]:
-            i, j = along(h, 0, m)
-            own = rows_ref.at[h, ctx_at(i, j)]
-            for k in range(1, major):
-                folds[h, k, m].wait_recv()
-                add_into(own, first_ref.at[h, k, m])
-            if m:
-                lasts[h, m] = send(
-                    own, second_ref.at[h, m], last_sem, (h, m), {"ctx": ctx_at(i, j)}
+    for r in range(pieces):
+        for h in range(2):
+            major, minor = along(h, wide, tall)
+            for m in range(1, minor):
+                i, j = along(h, 0, m)
+                own = rows_ref.at[h, ctx_at(i, j), some(r)]
+                for k in range(1, major):
+                    folds[h, k, m, r].wait_recv()
+                    add_into(own, first_ref.at[h, k, m, some(r)])
+                lasts[h, m, r] = send(
+                    own,
+                    second_ref.at[h, m, some(r)],
+                    last_sem,
+                    (h, m, r),
+                    {"ctx": ctx_at(i, j)},
                 )
-                lasts[h, m].start()
-    for h in range(2):
-        for m in range(1, sizes[1 - h]):
-            lasts[h, m].wait_recv()
-            add_into(rows_ref.at[h, me], second_ref.at[h, m])
-    for s in range(planes):
-        h, start = (s * width) // half, (s * width) % half
-        leaving[s] = rows_ref[h, me, :, start : start + width]
-    outward = []
-    for d in range(1, planes):
-        goal = lax.rem(z + d, planes)
-        outward.append(send(leaving.at[goal], out_ref.at[z], out_sem, (d,), {"exp": goal}))
-        outward[-1].start()
+                lasts[h, m, r].start()
+    outward = {}
+    for r in range(pieces):
+        for h in range(2):
+            own = rows_ref.at[h, me, some(r)]
+            for k in range(1, sizes[h]):
+                folds[h, k, 0, r].wait_recv()
+                add_into(own, first_ref.at[h, k, 0, some(r)])
+            for m in range(1, sizes[1 - h]):
+                lasts[h, m, r].wait_recv()
+                add_into(own, second_ref.at[h, m, some(r)])
+        for s in range(planes):
+            h, start = (s * width) // half, (s * width) % half
+            leaving[s, some(r)] = rows_ref[h, me, some(r), start : start + width]
+        for d in range(1, planes):
+            goal = lax.rem(z + d, planes)
+            outward[d, r] = send(
+                leaving.at[goal, some(r)],
+                out_ref.at[z, some(r)],
+                out_sem,
+                (d, r),
+                {"exp": goal},
+            )
+            outward[d, r].start()
     out_ref[z] = leaving[z]
-    for copy in outward:
+    for copy in outward.values():
         copy.wait_recv()
-    for copy in inward + outward + list(swaps.values()) + list(folds.values()):
-        copy.wait_send()
-    for copy in lasts.values():
-        copy.wait_send()
+    for group in (inward, outward, swaps, folds, lasts):
+        for copy in group.values():
+            copy.wait_send()
 
 
 def expert_rows(picked, gain, gate_here, up_here, down_here):
@@ -367,14 +387,14 @@
             pltpu.VMEM((2, most, count, half), jnp.bfloat16),
             pltpu.VMEM((planes, count, width), jnp.bfloat16),
             sems((3,)),
-            sems((2, planes)),
-            sems((2, 2, most)),
-            sems((2, 2, most, most)),
+            sems((2, planes, 2)),
+            sems((2, 2, most, 2)),
+            sems((2, 2, most, most, 2)),
+            sems((2, 2, wide, tall, 2)),
             sems((2, 2, wide, tall)),
-            sems((2, 2, wide, tall)),
-            sems((2, 2, most, most)),
-            sems((2, 2, most)),
-            sems((2, planes)),
+            sems((2, 2, most, most, 2)),
+            sems((2, 2, most, 2)),
+            sems((2, planes, 2)),
         ],
         compiler_params=pltpu.CompilerParams(
             collective_id=0, has_side_effects=True, vmem_limit_bytes=60 * 1024 * 1024
@@ -387,8 +407,119 @@
     )(picked, gain, gate_here, up_here, down_here)
 
 
-def join_states(earlier, later):
-    return (earlier[0] + later[0], jnp.exp(later[0])[:, None, None] * earlier[1] + later[1])
+def state_kernel(wide, tall, own_ref, all_ref, one_sem, two_sem, twin_sem):
+    me = lax.axis_index("ctx")
+    core = lax.rem(me, 2)
+    chip = me // 2
+    x, y = lax.rem(chip, wide), chip // wide
+    sizes = (wide, tall)
+
+    def ctx_at(i, j):
+        return (lax.rem(y + j + tall, tall) * wide + lax.rem(x + i + wide, wide)) * 2 + core
+
+    def send(block, sem, index, where):
+        return pltpu.make_async_remote_copy(
+            src_ref=block,
+            dst_ref=block,
+            send_sem=sem.at[(0,) + index],
+            recv_sem=sem.at[(1,) + index],
+            device_id=where,
+            device_id_type=MESH,
+        )
+
+    def along(h, first, second):
+        return (first, second) if h == 0 else (second, first)
+
+    twin = {"ctx": me + 1 - 2 * core}
+    partners = [twin]
+    partners += [{"ctx": ctx_at(i, 0)} for i in range(1, wide)]
+    partners += [{"ctx": ctx_at(0, j)} for j in range(1, tall)]
+    barrier = pltpu.get_barrier_semaphore()
+    for partner in partners:
+        pl.semaphore_signal(barrier, inc=1, device_id=partner, device_id_type=MESH)
+    for h in range(2):
+        all_ref[h, me] = own_ref[h]
+    pl.semaphore_wait(barrier, len(partners))
+    ones, twos, twins = {}, {}, {}
+    for h in range(2):
+        for k in range(1, sizes[h]):
+            i, j = along(h, k, 0)
+            ones[h, k] = send(all_ref.at[h, me], one_sem, (h, k), {"ctx": ctx_at(i, j)})
+            ones[h, k].start()
+
+    def pass_on(h, i, j):
+        twins[h, i, j] = send(all_ref.at[h, ctx_at(-i, -j)], twin_sem, (h, i, j), twin)
+        twins[h, i, j].start()
+
+    def turn(h, k):
+        i, j = along(h, k, 0)
+        block = all_ref.at[h, ctx_at(-i, -j)]
+        for m in range(1, sizes[1 - h]):
+            a, b = along(h, 0, m)
+            twos[h, k, m] = send(block, two_sem, (h, k, m), {"ctx": ctx_at(a, b)})
+            twos[h, k, m].start()
+
+    for h in range(2):
+        turn(h, 0)
+    for h in range(2):
+        pass_on(h, 0, 0)
+    for h in range(2):
+        for k in range(1, sizes[h]):
+            ones[h, k].wait_recv()
+            turn(h, k)
+            pass_on(h, *along(h, k, 0))
+    for k in range(max(sizes)):
+        for h in range(2):
+            if k < sizes[h]:
+                for m in range(1, sizes[1 - h]):
+                    twos[h, k, m].wait_recv()
+                    pass_on(h, *along(h, k, m))
+    for copy in twins.values():
+        copy.wait_recv()
+    for copy in list(ones.values()) + list(twos.values()) + list(twins.values()):
+        copy.wait_send()
+
+
+def states_before(overall, states):
+    shards, mine = lax.axis_size("ctx"), lax.axis_index("ctx")
+    wide = math.isqrt(shards // 2)
+    tall = shards // 2 // wide
+    most = max(wide, tall)
+    heads, head_width, nstate = states.shape
+    high = lax.reduce_precision(overall, 8, 7)
+    tail = jnp.zeros((16, nstate), jnp.float32)
+    tail = tail.at[0, :heads].set(high).at[1, :heads].set(overall - high)
+    own = jnp.concatenate(
+        [states.reshape(2, heads // 2 * head_width, nstate), jnp.stack([tail, tail])], axis=1
+    ).astype(jnp.bfloat16)
+    rows = own.shape[1]
+    sems = pltpu.SemaphoreType.DMA
+    vmem = pl.BlockSpec(memory_space=pltpu.VMEM)
+    gathered = pl.pallas_call(
+        functools.partial(state_kernel, wide, tall),
+        out_shape=jax.ShapeDtypeStruct((2, shards, rows, nstate), jnp.bfloat16),
+        in_specs=[vmem],
+        out_specs=vmem,
+        scratch_shapes=[
+            sems((2, 2, most)),
+            sems((2, 2, most, most)),
+            sems((2, 2, wide, tall)),
+        ],
+        compiler_params=pltpu.CompilerParams(
+            collective_id=1, has_side_effects=True, vmem_limit_bytes=40 * 1024 * 1024
+        ),
+    )(own)
+    logs = gathered[0, :, rows - 16 : rows - 14, :heads].astype(jnp.float32)
+    logs = logs[:, 0] + logs[:, 1]
+    index = jnp.arange(shards)
+    later = (index[None, :] > index[:, None]) & (index[None, :] < mine)
+    fade = jnp.exp(jnp.sum(jnp.where(later[:, :, None], logs[None], 0.0), axis=1))
+    fade = jnp.where((index < mine)[:, None], fade, 0.0)
+    fade = fade.reshape(shards, 2, heads // 2).transpose(1, 0, 2)
+    parts = gathered[:, :, : rows - 16].astype(jnp.float32)
+    parts = parts.reshape(2, shards, heads // 2, head_width, nstate)
+    before = jnp.sum(fade[:, :, :, None, None] * parts, axis=1)
+    return before.reshape(heads, head_width, nstate)
 
 
 def on_device(
@@ -413,10 +544,7 @@
     within, running, overall, states = local_block(
         ssm_input, key_proj, query_proj, step_size, decay_rate, head_count
     )
-    prefix = carried_in(
-        (overall, states), "ctx", join_states, (jnp.zeros_like(overall), jnp.zeros_like(states))
-    )
-    before = prefix[1]
+    before = states_before(overall, states)
     carried = jnp.einsum(
         "th,hpn,tn->thp",
         jnp.exp(running),

time: 184 us -> 140 us (0.76)
  waiting for transfers between devices: 18.5 us -> 0 us
  between operations: 14.3 us -> 0.95 us
  blocking collectives: 8.76 us -> 0 us
  other arithmetic: 10.7 us -> 3.26 us
  Pallas kernels: 121 us -> 127 us
    all_gather x1 -> x0, waiting for transfers between devices: 18.5 us -> none  [carried_in(): lax.all_gather(part.astype(kind), axis)]
    pallas_call x0 -> x1, Pallas kernels: none -> 13.7 us  [states_before(): pl.pallas_call(functools.partial(state_kernel, wide, tall), out_shape=jax...]
    select_n x8 -> x0, other arithmetic: 8.78 us -> none  [lap(): return jax.tree.map(lambda a, b: jnp.where(reached, a, b), new, before)]
    all_gather x1 -> x0, blocking collectives: 8.76 us -> none  [carried_in(): lax.all_gather(part.astype(kind), axis)]
    pallas_call x1, Pallas kernels: 121 us -> 113 us  [expert_rows(): pl.pallas_call(functools.partial(expert_kernel, wide, tall), out_shape=ja...]
  transfers between devices with their start and end apart: 1 -> 0, of which waited for: 1 -> 0; matrix products, arithmetic and copies ran while one was open for 1% -> 0% of each run, Pallas kernels for 0% -> 0%
where the time goes in v2:
time: 140 us
  Pallas kernels  127 us (91%)
  matrix products  5.91 us (4%)
  other arithmetic  3.26 us (2%)
  local copies, waits for them, and re-layouts  3.25 us (2%)
    pallas_call x1, Pallas kernels, expert_rows(): pl.pallas_call(functools.partial(expert_kernel, wide, tall), out_shape=ja...  113 us
    pallas_call x1, Pallas kernels, states_before(): pl.pallas_call(functools.partial(state_kernel, wide, tall), out_shape=jax...  13.7 us

profile of v2, /device:TPU:24, one launch (start us, length us, event | category | flops | bytes accessed | tf_op | source)
XLA Modules:
  0.0 139.9 jit_solution(10787245834714416680)
XLA Ops:
  0.6 0.0 copy-start
  0.6 0.8 negate_multiply_fusion
  1.4 0.1 copy.39
  1.5 0.2 reduce_window_sum.22
  1.7 0.1 copy.44
  1.8 1.1 copy.42
  2.9 0.0 copy-done
  2.9 0.4 convolution_convert_fusion.1
  3.4 0.2 scatter.9
  3.6 0.0 copy-start.4
  3.6 13.7 %shard_map.149 = bf16[2,8,528,128]{3,2,1,0:T(8,128)(2,1)S(1)} custom-call(bf16[2,528,128]{2,1,0:T(8,128)(2,1)S(1)} %maximum_maximum_fusion.own_ref), custom_call_target="tpu_custom_call" | custom-call | tf_op jit(solution)/shard_map/pallas_call | solution.py:498
  17.3 0.0 copy-start.2
  17.4 0.1 select_reduce_fusion
  17.5 0.1 exp.24
  17.5 0.1 select_bitcast_fusion
  17.6 0.1 mul.57
  17.7 0.1 mul.58
  17.8 1.3 multiply_reduce_fusion
  19.1 0.1 copy.43
  19.1 0.0 copy-done.4
  19.1 0.4 fusion.2
  19.5 0.1 copy.40
  19.6 0.0 copy-done.2
  19.6 0.2 convert_multiply_fusion
  19.7 0.2 copy.46
  19.9 0.1 fusion.29
  20.1 0.0 copy-start.3
  20.1 0.0 copy-start.6
  20.1 1.4 multiply_reduce_fusion.2
  21.5 0.0 copy-start.7
  21.5 0.0 copy-start.5
  21.6 0.2 copy.47
  21.8 0.0 copy-done.3
  21.8 0.0 copy-done.6
  21.8 0.1 add_convert_fusion
  21.9 0.3 copy-done.7
  22.2 0.0 copy-start.1
  22.2 0.3 reduce_window_sum.23
  22.5 0.1 eq.45
  22.6 0.1 convert_convert_fusion
  22.8 1.2 convolution_convert_fusion
  24.0 0.0 copy-done.5
  24.0 0.6 reshape.207.gain_ref
  24.6 0.0 copy-start.8
  24.6 112.8 %shard_map.150 = bf16[4,96,1024]{2,1,0:T(8,128)(2,1)} custom-call(bf16[4,96,1024]{2,1,0:T(8,128)(2,1)} %bitcast.59, f32[4,1024]{1,0:T(4,128)} %reshape.207.gain_ref, bf16[4096,1536]{1,0:T(8,128)(2,1)} %bitcast.62, bf16[4096,1536]{1,0:T(8,128)(2,1)} %bitcast.63, bf16[1536,4096]{1,0:T(8,128)(2,1)} %bitcast.64), custom_call_target="tpu_custom_call" | custom-call | flops 28991029248 | bytes 37748736 | tf_op jit(solution)/shard_map/pallas_call | solution.py:373
  137.4 0.0 copy-done.1
  137.4 0.0 copy-done.8
  137.5 2.4 %multiply_reduce_fusion.1 = bf16[128,1024]{1,0:T(8,128)(2,1)} fusion(bf16[4,96,1024]{2,1,0:T(8,128)(2,1)} %shard_map.150, f32[4,128]{1,0:T(4,128)S(1)} %select_reduce_fusion.1, s32[4,128]{1,0:T(4,128)S(1)} %broadcast_add_fusion, pred[4,128]{1,0:T(4,128)(4,1)S(1)} %get-tuple-element.28), kind=kOutput, calls=%fused_computation.1 | convolution fusion | flops 101777408 | bytes 1053184 | tf_op jit(solution)/shard_map/ekt,ekf->etf/dot_general | solution.py:580
  (20 shorter events, 0.2 us)
Async XLA Ops:
  0.6 2.3 %copy-start = (bf16[128,128]{1,0:T(8,128)(2,1)S(1)}, bf16[128,128]{1,0:T(8,128)(2,1)}, u32[]{:S(2)}) copy-start(bf16[128,128]{1,0:T(8,128)(2,1)} %param.20) | copy-start | bytes 98308
  3.6 15.5 %copy-start.4 = (bf16[128,128]{1,0:T(8,128)(2,1)S(1)}, bf16[128,128]{1,0:T(8,128)(2,1)}, u32[]{:S(2)}) copy-start(bf16[128,128]{1,0:T(8,128)(2,1)} %param.21) | copy-start | bytes 98308
  17.3 2.3 %copy-start.2 = (bf16[128,1024]{1,0:T(8,128)(2,1)S(1)}, bf16[128,1024]{1,0:T(8,128)(2,1)}, u32[]{:S(2)}) copy-start(bf16[128,1024]{1,0:T(8,128)(2,1)} %param.19) | copy-start | bytes 786436
  20.1 1.7 %copy-start.3 = (bf16[128,1024]{1,0:T(8,128)(2,1)S(1)}, bf16[128,1024]{1,0:T(8,128)(2,1)}, u32[]{:S(2)}) copy-start(bf16[128,1024]{1,0:T(8,128)(2,1)} %param.25) | copy-start | bytes 786436
  20.1 1.7 %copy-start.6 = (f32[1024]{0:T(1024)S(1)}, f32[1024]{0:T(1024)}, u32[]{:S(2)}) copy-start(f32[1024]{0:T(1024)} %param.24) | copy-start | bytes 12292
  21.5 0.7 copy-start.7
  21.5 2.5 %copy-start.5 = (f32[4096]{0:T(1024)S(1)}, f32[4096]{0:T(1024)}, u32[]{:S(2)}) copy-start(f32[4096]{0:T(1024)} %param.26) | copy-start | bytes 49156
  22.2 115.2 %copy-start.1 = (bf16[128,1024]{1,0:T(8,128)(2,1)}, bf16[128,1024]{1,0:T(8,128)(2,1)S(1)}, u32[]{:S(2)}) copy-start(bf16[128,1024]{1,0:T(8,128)(2,1)S(1)} %add_convert_fusion) | copy-start | bytes 786436
  24.6 112.8 %copy-start.8 = (f32[128,2]{0,1:T(2,128)S(1)}, f32[128,2]{0,1:T(2,128)}, u32[]{:S(2)}) copy-start(f32[128,2]{0,1:T(2,128)} %param.31) | copy-start | bytes 3076

commit v3 on v2

--- a/solution.py
+++ b/solution.py
@@ -105,6 +105,13 @@
     def along(h, first, second):
         return (first, second) if h == 0 else (second, first)
 
+    loads = [
+        pltpu.make_async_copy(gate_hbm, gate_ref, load_sem.at[0]),
+        pltpu.make_async_copy(up_hbm, up_ref, load_sem.at[1]),
+        pltpu.make_async_copy(down_hbm, down_ref, load_sem.at[2]),
+    ]
+    for load in loads:
+        load.start()
     twin = {"ctx": me + 1 - 2 * core}
     partners = [twin]
     partners += [{"ctx": ctx_at(i, 0)} for i in range(1, wide)]
@@ -130,13 +137,6 @@
                 {"exp": goal},
             )
             inward[d, r].start()
-    loads = [
-        pltpu.make_async_copy(gate_hbm, gate_ref, load_sem.at[0]),
-        pltpu.make_async_copy(up_hbm, up_ref, load_sem.at[1]),
-        pltpu.make_async_copy(down_hbm, down_ref, load_sem.at[2]),
-    ]
-    for load in loads:
-        load.start()
     arrived[z] = picked_ref[z]
     ones, twos, twins = {}, {}, {}
 
@@ -181,7 +181,8 @@
         for h in range(2):
             pass_on(h, 0, 0, r)
 
-    step = 256 if depth % 256 == 0 else 128
+    step = next(n for n in (512, 256, 128) if depth % n == 0)
+    lane = 512 if half % 512 == 0 else 256
 
     def raise_rows(i, j):
         group = j * wide + i
@@ -257,15 +258,15 @@
         base = chip_at(i, j) * 2
         for h in range(2):
 
-            @pl.loop(0, half // 256)
+            @pl.loop(0, half // lane)
             def _(t):
-                cols = pl.ds(pl.multiple_of(t * 256, 256), 256)
-                source = pl.ds(pl.multiple_of(h * half + t * 256, 256), 256)
+                cols = pl.ds(pl.multiple_of(t * lane, lane), lane)
+                source = pl.ds(pl.multiple_of(h * half + t * lane, lane), lane)
                 value = jnp.dot(
                     hidden_ref[group], down_ref[:, source], preferred_element_type=jnp.float32
                 )
                 rows_ref[h, pl.ds(base, 2), :, cols] = value.astype(jnp.bfloat16).reshape(
-                    2, count, 256
+                    2, count, lane
                 )
 
             swaps[h, i, j] = send(

time: 140 us -> 132 us (0.943)
  Pallas kernels: 127 us -> 118 us
    pallas_call x1, Pallas kernels: 113 us -> 105 us  [expert_rows(): pl.pallas_call(functools.partial(expert_kernel, wide, tall), out_shape=ja...]
where the time goes in v3:
time: 132 us
  Pallas kernels  118 us (89%)
  matrix products  5.91 us (4%)
  other arithmetic  3.26 us (2%)
  local copies, waits for them, and re-layouts  3.25 us (2%)
    pallas_call x1, Pallas kernels, expert_rows(): pl.pallas_call(functools.partial(expert_kernel, wide, tall), out_shape=ja...  105 us
    pallas_call x1, Pallas kernels, states_before(): pl.pallas_call(functools.partial(state_kernel, wide, tall), out_shape=jax...  13.7 us

profile of v3, /device:TPU:24, one launch (start us, length us, event | category | flops | bytes accessed | tf_op | source)
XLA Modules:
  0.0 131.8 jit_solution(12732590333392717649)
XLA Ops:
  0.6 0.0 copy-start
  0.6 0.8 negate_multiply_fusion
  1.4 0.1 copy.39
  1.5 0.2 reduce_window_sum.22
  1.7 0.1 copy.44
  1.8 1.1 copy.42
  2.9 0.0 copy-done
  2.9 0.4 convolution_convert_fusion.1
  3.4 0.2 scatter.9
  3.6 0.0 copy-start.4
  3.6 13.7 %shard_map.149 = bf16[2,8,528,128]{3,2,1,0:T(8,128)(2,1)S(1)} custom-call(bf16[2,528,128]{2,1,0:T(8,128)(2,1)S(1)} %maximum_maximum_fusion.own_ref), custom_call_target="tpu_custom_call" | custom-call | tf_op jit(solution)/shard_map/pallas_call | solution.py:499
  17.3 0.0 copy-start.2
  17.4 0.1 select_reduce_fusion
  17.5 0.1 exp.24
  17.5 0.1 select_bitcast_fusion
  17.6 0.1 mul.57
  17.7 0.1 mul.58
  17.8 1.3 multiply_reduce_fusion
  19.1 0.1 copy.43
  19.1 0.0 copy-done.4
  19.1 0.4 fusion.2
  19.5 0.1 copy.40
  19.6 0.0 copy-done.2
  19.6 0.2 convert_multiply_fusion
  19.7 0.2 copy.46
  19.9 0.1 fusion.29
  20.1 0.0 copy-start.3
  20.1 0.0 copy-start.6
  20.1 1.4 %multiply_reduce_fusion.2 = (f32[128,16]{0,1:T(8,128)S(1)}, f32[128,16,64]{0,2,1:T(8,128)S(1)}) fusion(f32[128,16,64]{0,2,1:T(8,128)S(1)} %bitcast.60, f32[128,16,64]{0,2,1:T(8,128)S(1)} %fusion.2, bf16[128,16,64]{0,2,1:T(8,128)(2,1)S(1)} %bitcast.57, f32[128,128]{1,0:T(8,128)S(1)} %fusion.29, f32[128,16]{0,1:T(8,128)S(1)} %copy.40, ...), kind=kOutput, calls=%fused_computation.20 | convolution fusion | flops 202897408 | bytes 1933312 | tf_op jit(solution)/shard_map/tsh,ts,shp->thp/dot_general | solution.py:26
  21.5 0.0 copy-start.7
  21.5 0.0 copy-start.5
  21.6 0.2 copy.47
  21.8 0.0 copy-done.3
  21.8 0.0 copy-done.6
  21.8 0.1 add_convert_fusion
  21.9 0.3 copy-done.7
  22.2 0.0 copy-start.1
  22.2 0.3 reduce_window_sum.23
  22.6 0.1 eq.45
  22.6 0.1 convert_convert_fusion
  22.8 1.2 convolution_convert_fusion
  24.0 0.0 copy-done.5
  24.0 0.6 reshape.207.gain_ref
  24.6 0.0 copy-start.8
  24.6 104.7 %shard_map.150 = bf16[4,96,1024]{2,1,0:T(8,128)(2,1)} custom-call(bf16[4,96,1024]{2,1,0:T(8,128)(2,1)} %bitcast.59, f32[4,1024]{1,0:T(4,128)} %reshape.207.gain_ref, bf16[4096,1536]{1,0:T(8,128)(2,1)} %bitcast.62, bf16[4096,1536]{1,0:T(8,128)(2,1)} %bitcast.63, bf16[1536,4096]{1,0:T(8,128)(2,1)} %bitcast.64), custom_call_target="tpu_custom_call" | custom-call | flops 28991029248 | bytes 37748736 | tf_op jit(solution)/shard_map/pallas_call | solution.py:374
  129.4 0.0 copy-done.1
  129.4 0.0 copy-done.8
  129.4 2.4 %multiply_reduce_fusion.1 = bf16[128,1024]{1,0:T(8,128)(2,1)} fusion(bf16[4,96,1024]{2,1,0:T(8,128)(2,1)} %shard_map.150, f32[4,128]{1,0:T(4,128)S(1)} %select_reduce_fusion.1, s32[4,128]{1,0:T(4,128)S(1)} %broadcast_add_fusion, pred[4,128]{1,0:T(4,128)(4,1)S(1)} %get-tuple-element.28), kind=kOutput, calls=%fused_computation.1 | convolution fusion | flops 101777408 | bytes 1053184 | tf_op jit(solution)/shard_map/ekt,ekf->etf/dot_general | solution.py:581
  (20 shorter events, 0.2 us)
Async XLA Ops:
  0.6 2.3 %copy-start = (bf16[128,128]{1,0:T(8,128)(2,1)S(1)}, bf16[128,128]{1,0:T(8,128)(2,1)}, u32[]{:S(2)}) copy-start(bf16[128,128]{1,0:T(8,128)(2,1)} %param.20) | copy-start | bytes 98308
  3.6 15.5 %copy-start.4 = (bf16[128,128]{1,0:T(8,128)(2,1)S(1)}, bf16[128,128]{1,0:T(8,128)(2,1)}, u32[]{:S(2)}) copy-start(bf16[128,128]{1,0:T(8,128)(2,1)} %param.21) | copy-start | bytes 98308
  17.3 2.3 %copy-start.2 = (bf16[128,1024]{1,0:T(8,128)(2,1)S(1)}, bf16[128,1024]{1,0:T(8,128)(2,1)}, u32[]{:S(2)}) copy-start(bf16[128,1024]{1,0:T(8,128)(2,1)} %param.19) | copy-start | bytes 786436
  20.1 1.7 %copy-start.3 = (bf16[128,1024]{1,0:T(8,128)(2,1)S(1)}, bf16[128,1024]{1,0:T(8,128)(2,1)}, u32[]{:S(2)}) copy-start(bf16[128,1024]{1,0:T(8,128)(2,1)} %param.25) | copy-start | bytes 786436
  20.1 1.7 %copy-start.6 = (f32[1024]{0:T(1024)S(1)}, f32[1024]{0:T(1024)}, u32[]{:S(2)}) copy-start(f32[1024]{0:T(1024)} %param.24) | copy-start | bytes 12292
  21.5 0.7 copy-start.7
  21.5 2.5 %copy-start.5 = (f32[4096]{0:T(1024)S(1)}, f32[4096]{0:T(1024)}, u32[]{:S(2)}) copy-start(f32[4096]{0:T(1024)} %param.26) | copy-start | bytes 49156
  22.2 107.2 %copy-start.1 = (bf16[128,1024]{1,0:T(8,128)(2,1)}, bf16[128,1024]{1,0:T(8,128)(2,1)S(1)}, u32[]{:S(2)}) copy-start(bf16[128,1024]{1,0:T(8,128)(2,1)S(1)} %add_convert_fusion) | copy-start | bytes 786436
  24.6 104.8 %copy-start.8 = (f32[128,2]{0,1:T(2,128)S(1)}, f32[128,2]{0,1:T(2,128)}, u32[]{:S(2)}) copy-start(f32[128,2]{0,1:T(2,128)} %param.31) | copy-start | bytes 3076
